TPU v7x, 32 devices: a whole 2x2x4 slice. The times are simulated.
32 devices in a mesh: dp: 2 (over x), seq: 16 (over z, y, core).
Axes of the slice: x: 2, y: 2, z: 4, core: 2. Of those that a mesh axis runs over, the one named last changes fastest.
Arguments:
- queries: bfloat16 [2, 2048, 2048], P('dp', 'seq'), may hold values from -6 to 6
- keys: bfloat16 [2, 2048, 2048], P('dp', 'seq'), may hold values from -0.75 to 0.75
- values: bfloat16 [2, 2048, 2048], P('dp', 'seq'), may hold values from -6 to 6
- log_decay: float32 [2, 32, 2048], P('dp', None, 'seq'), may hold values from -0.7 to 0
- gain: float32 [2048], replicated, may hold values from 0.25 to 1.75
- d_out: bfloat16 [2, 2048, 2048], P('dp', 'seq'), may hold values from -12 to 12
Outputs:
- d_queries: bfloat16 [2, 2048, 2048], P('dp', 'seq')
- d_keys: bfloat16 [2, 2048, 2048], P('dp', 'seq')
- d_values: bfloat16 [2, 2048, 2048], P('dp', 'seq')
- d_log_decay: float32 [2, 32, 2048], P('dp', None, 'seq')
- d_gain: float32 [2048], replicated
All inputs are finite; a program needn't handle non-finite values.
Results may differ from a plain program's by a relative error of at most 0.001.
Values sent between devices are 32-bit elements; how exact they have to be, the bound alone decides.
A program may use at most 192 MiB of HBM per device.

v0:
```python
import jax
import jax.numpy as jnp
from jax import lax
from jax.sharding import PartitionSpec as P

HIGH = lax.Precision.HIGHEST
EPSILON = 1e-06


def decay_table(log_block):
    cumulative = jnp.cumsum(log_block, axis=1)
    spread = cumulative[:, :, None] - cumulative[:, None, :]
    length = log_block.shape[1]
    lower = jnp.arange(length)[:, None] >= jnp.arange(length)[None, :]
    table = jnp.where(lower[None], jnp.exp(jnp.minimum(spread, 0.0)), 0.0)
    return (cumulative, table)


def block_out(query, keys, values, log_block, start_state):
    cumulative, table = decay_table(log_block)
    scores = jnp.einsum("hdt,hds->hts", query, keys, precision=HIGH) * table
    inside = jnp.einsum("hts,hes->het", scores, values, precision=HIGH)
    carried = jnp.einsum("hdt,hde->het", query, start_state, precision=HIGH)
    return inside + jnp.exp(cumulative)[:, None, :] * carried


def block_end(keys, values, log_block, start_state):
    cumulative = jnp.cumsum(log_block, axis=1)
    total = cumulative[:, -1]
    weighted = keys * jnp.exp(total[:, None] - cumulative)[:, None, :]
    fresh = jnp.einsum("hds,hes->hde", weighted, values, precision=HIGH)
    return jnp.exp(total)[:, None, None] * start_state + fresh


def normalize(attended, gain):
    heads, width, length = attended.shape
    scale = jnp.sqrt(jnp.mean(attended * attended, axis=(0, 1)) + EPSILON)
    return attended / scale[None, None, :] * gain.reshape(heads, width, 1)


def running(states, rates):
    count = states.shape[0]
    hop = 1
    while hop < count:
        before_states = jnp.concatenate([jnp.zeros_like(states[:hop]), states[:-hop]], axis=0)
        before_rates = jnp.concatenate([jnp.ones_like(rates[:hop]), rates[:-hop]], axis=0)
        states = rates[:, :, None] * before_states + states
        rates = rates * before_rates
        hop = hop * 2
    return jnp.concatenate([jnp.zeros_like(states[:1]), states[:-1]], axis=0)


def rows_prefix(state, decay_speed, backward):
    count = lax.axis_size("seq")
    heads, width, _ = state.shape
    rows = heads * width // count
    laid = state.reshape(count, 1, rows, width)
    spread = jnp.repeat(decay_speed, width).reshape(count, 1, rows)
    if backward:
        flipped = running(
            jnp.flip(lax.all_to_all(laid, "seq", split_axis=0, concat_axis=1, tiled=True)[0], 0),
            jnp.flip(lax.all_to_all(spread, "seq", split_axis=0, concat_axis=1, tiled=True)[0], 0),
        )
        moved = lax.all_to_all(
            jnp.flip(flipped, 0)[None], "seq", split_axis=1, concat_axis=0, tiled=True
        )
    else:
        moved = lax.all_to_all(
            running(
                lax.all_to_all(laid, "seq", split_axis=0, concat_axis=1, tiled=True)[0],
                lax.all_to_all(spread, "seq", split_axis=0, concat_axis=1, tiled=True)[0],
            )[None],
            "seq",
            split_axis=1,
            concat_axis=0,
            tiled=True,
        )
    return moved.reshape(heads, width, width)


def shards(queries, keys, values, log_decay, gain, d_out):
    length = queries.shape[1]
    heads = log_decay.shape[1]
    width = queries.shape[2] // heads

    def split_heads(array):
        return jnp.transpose(array[0].reshape(length, heads, width), (1, 2, 0)).astype(jnp.float32)

    def merge_heads(array):
        return jnp.transpose(array.astype(jnp.bfloat16), (2, 0, 1)).reshape(length, heads * width)[
            None
        ]

    query_heads = split_heads(queries)
    key_heads = split_heads(keys)
    value_heads = split_heads(values)
    cotangent = split_heads(d_out)
    log_block = log_decay[0]
    decay_whole = jnp.exp(jnp.sum(log_block, axis=1))
    empty = jnp.zeros((heads, width, width), jnp.float32)
    fresh = block_end(key_heads, value_heads, log_block, empty)
    start_state = rows_prefix(fresh, decay_whole, False)

    def attend(query_in, key_in, value_in, log_in, state_in, gain_in):
        return normalize(block_out(query_in, key_in, value_in, log_in, state_in), gain_in)

    _, pull = jax.vjp(attend, query_heads, key_heads, value_heads, log_block, start_state, gain)
    d_query, d_key_inside, d_value_inside, d_log_inside, incoming, d_gain_local = pull(cotangent)
    end_grad = rows_prefix(incoming, decay_whole, True)

    def finish(key_in, value_in, log_in):
        return block_end(key_in, value_in, log_in, start_state)

    _, pull_end = jax.vjp(finish, key_heads, value_heads, log_block)
    d_key_carried, d_value_carried, d_log_carried = pull_end(end_grad)
    d_gain = lax.psum(d_gain_local, ("dp", "seq"))
    d_keys = merge_heads(d_key_inside + d_key_carried)
    d_values = merge_heads(d_value_inside + d_value_carried)
    d_log_decay = (d_log_inside + d_log_carried)[None]
    return (merge_heads(d_query), d_keys, d_values, d_log_decay, d_gain)


def solution(mesh):
    placed = (
        P("dp", "seq", None),
        P("dp", "seq", None),
        P("dp", "seq", None),
        P("dp", None, "seq"),
        P(),
        P("dp", "seq", None),
    )
    return jax.shard_map(
        shards,
        mesh=mesh,
        in_specs=placed,
        out_specs=(
            P("dp", "seq", None),
            P("dp", "seq", None),
            P("dp", "seq", None),
            P("dp", None, "seq"),
            P(),
        ),
        check_vma=False,
    )
```

profile of v0, /device:TPU:1, one launch (start us, length us, event | category | flops | bytes accessed | tf_op | source)
XLA Modules:
  0.0 173.6 jit_solution(10147940836437937576)
XLA Ops:
  0.6 0.8 reduce_sum.104
  1.5 0.1 exp.47
  1.6 0.1 broadcast_in_dim.32
  1.6 0.7 broadcast_in_dim.33
  2.3 7.3 %all-to-all-start = ((f32[16,1,128]{2,1,0:T(1,128)}), f32[16,1,128]{2,1,0:T(1,128)S(1)}, u32[]{:S(2)}, u32[]{:S(2)}) async-start(f32[16,1,128]{2,1,0:T(1,128)} %broadcast_in_dim.33), calls=%async_computation | async-start | bytes 16384 | tf_op jit(solution)/shard_map/all_to_all | solution.py:71
  9.7 1.0 reduce_window_sum.33
  10.7 0.1 copy.107
  10.9 1.3 copy.108
  12.2 1.3 copy.111
  13.6 0.9 convolution_add_fusion
  14.5 1.1 copy.112
  15.6 6.0 %all-to-all-start.1 = ((f32[16,1,128,64]{2,3,1,0:T(8,128)}), f32[16,1,128,64]{2,3,1,0:T(8,128)S(1)}, u32[]{:S(2)}, u32[]{:S(2)}) async-start(f32[16,1,128,64]{2,3,1,0:T(8,128)} %copy.112), calls=%async_computation.1 | async-start | bytes 1048576 | tf_op jit(solution)/shard_map/all_to_all | solution.py:70
  21.7 14.0 %all-to-all-done.1 = f32[16,1,128,64]{2,3,1,0:T(8,128)S(1)} async-done(((f32[16,1,128,64]{2,3,1,0:T(8,128)}), f32[16,1,128,64]{2,3,1,0:T(8,128)S(1)}, u32[]{:S(2)}, u32[]{:S(2)}) %all-to-all-start.1) | async-done | bytes 524320 | tf_op jit(solution)/shard_map/all_to_all | solution.py:70
  35.8 0.1 bitcast_add_fusion
  35.9 0.1 multiply_add_fusion.3
  36.0 0.1 multiply_add_fusion.2
  36.2 0.8 pad_bitcast_fusion
  37.1 4.5 %all-to-all-start.2 = ((f32[1,16,128,64]{2,3,0,1:T(8,128)}), f32[1,16,128,64]{2,3,0,1:T(8,128)}, u32[]{:S(2)}, u32[]{:S(2)}) async-start(f32[1,16,128,64]{2,3,0,1:T(8,128)} %pad_bitcast_fusion), calls=%async_computation.2 | async-start | bytes 1048576 | tf_op jit(solution)/shard_map/all_to_all | solution.py:68
  41.6 0.1 mul.225
  41.6 0.3 copy.117
  41.9 0.2 copy.116
  42.2 1.8 %fusion.70 = f32[32,128,128]{2,1,0:T(8,128)} fusion(bf16[32,64,128]{2,1,0:T(8,128)(2,1)S(1)} %bitcast.120, bf16[32,64,128]{2,1,0:T(8,128)(2,1)S(1)} %bitcast.110), kind=kOutput, calls=%fused_computation.99 | convolution fusion | flops 67108864 | bytes 3145728 | tf_op jit(solution)/shard_map/jvp(hdt,hds->hts)/dot_general | solution.py:21
  44.0 11.7 %all-to-all-done.2 = f32[1,16,128,64]{2,3,0,1:T(8,128)} async-done(((f32[1,16,128,64]{2,3,0,1:T(8,128)}), f32[1,16,128,64]{2,3,0,1:T(8,128)}, u32[]{:S(2)}, u32[]{:S(2)}) %all-to-all-start.2) | async-done | bytes 524320 | tf_op jit(solution)/shard_map/all_to_all | solution.py:68
  55.8 1.4 copy.134
  57.2 1.0 fusion.71
  58.2 0.6 copy-done.1
  58.7 0.1 copy-done.3
  58.8 2.4 %multiply_reduce_fusion.3 = (f32[128]{0:T(128)S(1)}, f32[32,64,128]{2,1,0:T(8,128)S(1)}) fusion(f32[32,64,128]{2,1,0:T(8,128)S(1)} %fusion.71, f32[32,128]{1,0:T(8,128)S(1)} %exp.50, bf16[32,64,128]{2,1,0:T(8,128)(2,1)S(1)} %bitcast.126, f32[32,128,128]{2,1,0:T(8,128)S(1)} %copy-done.1, f32[32,128]{1,0:T(8,128)S(1)} %reduce_window_sum.33, ...), kind=kOutput, calls=%fused_computation.35 | convolution fusion | flops 405798784 | bytes 4768256 | tf_op jit(solution)/shard_map/jvp(hts,hes->het)/dot_general | solution.py:22
  61.2 0.7 multiply_reduce_fusion
  61.9 1.7 multiply_reduce_fusion.1
  63.6 0.9 convolution_bitcast_fusion.1
  64.5 1.6 copy.120
  66.1 2.2 %reshape.190 = f32[16,1,128,64]{2,0,3,1:T(8,128)} reshape(f32[32,64,64]{1,0,2:T(8,128)} %copy.120) | data formatting | bytes 1048576 | tf_op jit(solution)/shard_map/reshape | solution.py:57
  68.4 2.0 %copy.121 = f32[16,1,128,64]{2,3,1,0:T(8,128)} copy(f32[16,1,128,64]{2,0,3,1:T(8,128)} %reshape.190) | data formatting | bytes 1048576 | tf_op jit(solution)/shard_map/reshape | solution.py:57
  70.4 4.5 %all-to-all-start.3 = ((f32[16,1,128,64]{2,3,1,0:T(8,128)}), f32[16,1,128,64]{2,3,1,0:T(8,128)}, u32[]{:S(2)}, u32[]{:S(2)}) async-start(f32[16,1,128,64]{2,3,1,0:T(8,128)} %copy.121), calls=%async_computation.3 | async-start | bytes 1048576 | tf_op jit(solution)/shard_map/all_to_all | solution.py:61
  75.0 14.1 %all-to-all-done.3 = f32[16,1,128,64]{2,3,1,0:T(8,128)} async-done(((f32[16,1,128,64]{2,3,1,0:T(8,128)}), f32[16,1,128,64]{2,3,1,0:T(8,128)}, u32[]{:S(2)}, u32[]{:S(2)}) %all-to-all-start.3) | async-done | bytes 524320 | tf_op jit(solution)/shard_map/all_to_all | solution.py:61
  89.1 1.9 %slice_bitcast_fusion = f32[15,128,64]{1,2,0:T(8,128)} fusion(f32[16,1,128,64]{2,3,0,1:T(8,128)} %bitcast.28), kind=kLoop, calls=%fused_computation.69 | loop fusion | bytes 983040 | tf_op jit(solution)/shard_map/slice | solution.py:45
  90.9 1.9 %slice.89 = f32[15,128,64]{1,2,0:T(8,128)} reverse(f32[15,128,64]{1,2,0:T(8,128)} %slice_bitcast_fusion), dimensions={0} | reverse | bytes 983040 | tf_op jit(solution)/shard_map/slice | solution.py:45
  92.8 1.3 reverse_add_fusion
  94.1 0.1 multiply_add_fusion.1
  94.2 0.1 multiply_add_fusion
  94.3 0.1 slice_add_fusion
  94.4 0.8 reverse_bitcast_fusion
  95.2 4.5 %all-to-all-start.4 = ((f32[1,16,128,64]{2,3,0,1:T(8,128)}), f32[1,16,128,64]{2,3,0,1:T(8,128)}, u32[]{:S(2)}, u32[]{:S(2)}) async-start(f32[1,16,128,64]{2,3,0,1:T(8,128)} %reverse_bitcast_fusion), calls=%async_computation.4 | async-start | bytes 1048576 | tf_op jit(solution)/shard_map/all_to_all | solution.py:64
  99.7 5.5 %fusion.69 = (f32[32,128]{1,0:T(8,128)S(1)}, f32[32,128]{1,0:T(8,128)S(1)}, f32[32,128,128]{2,1,0:T(8,128)}) fusion(f32[32,128]{1,0:T(8,128)S(1)} %reduce_window_sum.33, f32[32,128,128]{2,1,0:T(8,128)} %fusion.70, f32[32,64,128]{2,1,0:T(8,128)S(1)} %get-tuple-element.40, bf16[32,64,128]{2,1,0:T(8,128)(2,1)} %bitcast.125, ...), kind=kOutput, calls=%fused_computation.98 | convolution fusion | flops 408936448 | bytes 5832704 | tf_op jit(solution)/shard_map/transpose(jvp(hts,hes->het))/dot_general | solution.py:22
  105.2 0.1 reshape.193
  105.3 1.2 reduce_window_sum.34
  106.5 4.0 %fusion.14 = f32[128,32,64]{0,2,1:T(8,128)S(1)} fusion(bf16[32,64,128]{2,1,0:T(8,128)(2,1)S(1)} %bitcast.111, f32[32,128,128]{2,1,0:T(8,128)} %get-tuple-element.47, f32[32,128]{1,0:T(8,128)S(1)} %reduce_window_sum.33, pred[128,128]{1,0:T(8,128)(4,1)S(1)} %iota_compare_fusion), kind=kOutput, calls=%fused_computation.14 | convolution fusion | flops 404750336 | bytes 3702784 | tf_op jit(solution)/shard_map/transpose(jvp(hdt,hds->hts))/dot_general | solution.py:21
  110.5 2.0 %fusion.36 = bf16[128,32,64]{0,2,1:T(8,128)(2,1)} fusion(f32[128,32,64]{0,2,1:T(8,128)S(1)} %fusion.14, f32[32,64,64]{2,1,0:T(8,128)S(1)} %bitcast.115, f32[32,64,128]{2,1,0:T(8,128)S(1)} %get-tuple-element.40, f32[32,128]{1,0:T(8,128)S(1)} %exp.50), kind=kOutput, calls=%fused_computation.27 | convolution fusion | flops 202113024 | bytes 3162112 | tf_op jit(solution)/shard_map/transpose(jvp(hdt,hde->het))/dot_general | solution.py:23
  112.5 2.0 %copy.129 = bf16[1,128,2048]{2,1,0:T(8,128)(2,1)} copy(bf16[1,128,2048]{1,2,0:T(8,128)(2,1)} %bitcast.130) | data formatting | bytes 1048576
  114.6 39.9 %psum.7 = f32[2048]{0:T(1024)} all-reduce(f32[2048]{0:T(1024)S(1)} %reshape.193), channel_id=1, replica_groups=mesh['dp'=2,'seq'=16] {'dp','seq'}, use_global_device_ids=true, to_apply=%region_14.15 | all-reduce | flops 2048 | bytes 16384 | tf_op jit(solution)/shard_map/psum | solution.py:116
  154.5 1.4 copy.124
  155.9 2.8 %fusion.40 = f32[32,64,128]{2,1,0:T(8,128)} fusion(f32[32,64,64]{2,1,0:T(8,128)S(1)} %bitcast.118, bf16[32,64,128]{2,1,0:T(8,128)(2,1)S(1)} %bitcast.112, f32[32,128]{1,0:T(8,128)S(1)} %copy.110), kind=kOutput, calls=%fused_computation.29 | convolution fusion | flops 201850880 | bytes 2113536 | tf_op jit(solution)/shard_map/transpose(jvp(hds,hes->hde))/dot_general | solution.py:31
  158.7 1.7 fusion.41
  160.4 1.3 multiply_reduce_fusion.4
  161.7 0.1 reduce_sum.118
  161.8 0.1 reduce_sum.136
  161.9 4.3 %fusion.37 = bf16[32,64,128]{2,1,0:T(8,128)(2,1)S(1)} fusion(f32[32,64,128]{2,1,0:T(8,128)} %fusion.40, f32[32,64,128]{2,1,0:T(8,128)S(1)} %get-tuple-element.40, f32[32,128,128]{2,1,0:T(8,128)} %fusion.70, f32[32,128]{1,0:T(8,128)S(1)} %reduce_window_sum.33, pred[128,128]{1,0:T(8,128)(4,1)S(1)} %iota_compare_fusion), kind=kOutput, calls=%fused_computation.28 | convolution fusion | flops 405274624 | bytes 4751360 | tf_op jit(solution)/shard_map/transpose(jvp(hts,hes->het))/dot_general | solution.py:22
  166.2 1.0 copy.131
  167.3 3.2 %fusion.33 = bf16[128,32,64]{0,2,1:T(8,128)(2,1)S(1)} fusion(bf16[32,64,128]{2,1,0:T(8,128)(2,1)S(1)} %bitcast.123, f32[32,128,128]{2,1,0:T(8,128)} %get-tuple-element.47, f32[32,64,128]{2,1,0:T(8,128)S(1)} %copy-done.5, f32[32,128]{1,0:T(8,128)S(1)} %reduce_window_sum.33, pred[128,128]{1,0:T(8,128)(4,1)S(1)} %iota_compare_fusion, f32[128,32]{0,1:T(8,128)S(1)} %copy.125), kind=kOutput, calls=%fused_computation.26 | convolution fusion | flops 405536768 | bytes 4243456 | tf_op jit(solution)/shard_map/transpose(jvp(hdt,hds->hts))/dot_general | solution.py:21
  170.5 1.0 copy.130
  171.5 0.1 copy.127
  171.7 1.3 reduce_window_sum.36
  173.0 0.6 add.112
  (54 shorter events, 0.8 us)
Async XLA Ops:
  2.3 13.3 %all-to-all-start = ((f32[16,1,128]{2,1,0:T(1,128)}), f32[16,1,128]{2,1,0:T(1,128)S(1)}, u32[]{:S(2)}, u32[]{:S(2)}) async-start(f32[16,1,128]{2,1,0:T(1,128)} %broadcast_in_dim.33), calls=%async_computation | async-start | bytes 16384 | tf_op jit(solution)/shard_map/all_to_all | solution.py:71
  13.6 2.1 %copy-start.2 = (bf16[1,128,2048]{1,2,0:T(8,128)(2,1)}, bf16[1,128,2048]{1,2,0:T(8,128)(2,1)S(1)}, u32[]{:S(2)}) copy-start(bf16[1,128,2048]{1,2,0:T(8,128)(2,1)S(1)} %copy.111) | copy-start | bytes 1572868
  15.6 20.1 %all-to-all-start.1 = ((f32[16,1,128,64]{2,3,1,0:T(8,128)}), f32[16,1,128,64]{2,3,1,0:T(8,128)S(1)}, u32[]{:S(2)}, u32[]{:S(2)}) async-start(f32[16,1,128,64]{2,3,1,0:T(8,128)} %copy.112), calls=%async_computation.1 | async-start | bytes 1048576 | tf_op jit(solution)/shard_map/all_to_all | solution.py:70
  36.1 5.5 %copy-start.8 = (f32[2048]{0:T(1024)S(1)}, f32[2048]{0:T(1024)}, u32[]{:S(2)}) copy-start(f32[2048]{0:T(1024)} %param.10) | copy-start | bytes 24580
  36.1 5.5 %copy-start.7 = (bf16[1,128,2048]{2,1,0:T(8,128)(2,1)S(1)}, bf16[1,128,2048]{2,1,0:T(8,128)(2,1)}, u32[]{:S(2)}) copy-start(bf16[1,128,2048]{2,1,0:T(8,128)(2,1)} %param.6) | copy-start | bytes 1572868
  36.1 5.8 %copy-start.6 = (bf16[1,128,2048]{2,1,0:T(8,128)(2,1)S(1)}, bf16[1,128,2048]{2,1,0:T(8,128)(2,1)}, u32[]{:S(2)}) copy-start(bf16[1,128,2048]{2,1,0:T(8,128)(2,1)} %param.11) | copy-start | bytes 1572868
  37.1 18.7 %all-to-all-start.2 = ((f32[1,16,128,64]{2,3,0,1:T(8,128)}), f32[1,16,128,64]{2,3,0,1:T(8,128)}, u32[]{:S(2)}, u32[]{:S(2)}) async-start(f32[1,16,128,64]{2,3,0,1:T(8,128)} %pad_bitcast_fusion), calls=%async_computation.2 | async-start | bytes 1048576 | tf_op jit(solution)/shard_map/all_to_all | solution.py:68
  42.1 19.1 %copy-start = (f32[1,128,2048]{1,2,0:T(8,128)}, f32[1,128,2048]{1,2,0:T(8,128)S(1)}, u32[]{:S(2)}) copy-start(f32[1,128,2048]{1,2,0:T(8,128)S(1)} %copy.116) | copy-start | bytes 3145732
  57.1 1.6 copy-start.1
  57.2 1.7 copy-start.3
  70.4 18.7 %all-to-all-start.3 = ((f32[16,1,128,64]{2,3,1,0:T(8,128)}), f32[16,1,128,64]{2,3,1,0:T(8,128)}, u32[]{:S(2)}, u32[]{:S(2)}) async-start(f32[16,1,128,64]{2,3,1,0:T(8,128)} %copy.121), calls=%async_computation.3 | async-start | bytes 1048576 | tf_op jit(solution)/shard_map/all_to_all | solution.py:61
  95.2 59.3 %all-to-all-start.4 = ((f32[1,16,128,64]{2,3,0,1:T(8,128)}), f32[1,16,128,64]{2,3,0,1:T(8,128)}, u32[]{:S(2)}, u32[]{:S(2)}) async-start(f32[1,16,128,64]{2,3,0,1:T(8,128)} %reverse_bitcast_fusion), calls=%async_computation.4 | async-start | bytes 1048576 | tf_op jit(solution)/shard_map/all_to_all | solution.py:64
  155.9 2.9 %copy-start.4 = (bf16[1,128,2048]{1,2,0:T(8,128)(2,1)S(1)}, bf16[1,128,2048]{1,2,0:T(8,128)(2,1)}, u32[]{:S(2)}) copy-start(bf16[1,128,2048]{1,2,0:T(8,128)(2,1)} %copy-done.2) | copy-start | bytes 1572868
  161.9 5.4 %copy-start.5 = (f32[32,64,128]{2,1,0:T(8,128)S(1)}, f32[32,64,128]{2,1,0:T(8,128)}, u32[]{:S(2)}) copy-start(f32[32,64,128]{2,1,0:T(8,128)} %get-tuple-element.49) | copy-start | bytes 3145732
where the time goes:
time: 176 us; the launch traced here: 174 us
  blocking collectives  39.9 us (23%)
  waiting for transfers between devices  39.8 us (23%)
  matrix products  30.7 us (17%)
  starting transfers between devices  26.8 us (15%)
  local copies, waits for them, and re-layouts  24.7 us (14%)
  other arithmetic  10.6 us (6%)
    psum x1, blocking collectives, shards(): d_gain = lax.psum(d_gain_local, ('dp', 'seq'))  39.9 us
    all_to_all x2, waiting for transfers between devices, rows_prefix(): lax.all_to_all(laid, 'seq', split_axis=0, concat_axis=1, tiled=True)[0]  28.1 us
    dot_general x3, matrix products, block_out(): inside = jnp.einsum('hts,hes->het', scores, values, precision=HIGH)  12.2 us
    all_to_all x1, waiting for transfers between devices, rows_prefix(): lax.all_to_all(running(lax.all_to_all(laid, 'seq', split_axis=0, concat_a...  11.7 us
    all_to_all x2, starting transfers between devices, rows_prefix(): lax.all_to_all(laid, 'seq', split_axis=0, concat_axis=1, tiled=True)[0]  10.5 us
    dot_general x3, matrix products, block_out(): scores = jnp.einsum('hdt,hds->hts', query, keys, precision=HIGH) * table  8.99 us
    unnamed x25, local copies, waits for them, and re-layouts  7.66 us
    all_to_all x1, starting transfers between devices, rows_prefix(): lax.all_to_all(spread, 'seq', split_axis=0, concat_axis=1, tiled=True)[0]  7.35 us
  transfers between devices with their start and end apart: 5, of which 3 were waited for; matrix products, arithmetic and copies ran while one was open for 13% of the time, Pallas kernels for 0%

commit v1 on v0

v1 whole, which is shorter than its diff:
```python
import functools

import jax
import jax.numpy as jnp
from jax import lax
from jax.experimental import pallas as pl
from jax.experimental.pallas import tpu as pltpu
from jax.sharding import PartitionSpec as P

EPSILON = 1e-06
HIGH = lax.Precision.HIGHEST
F32 = jnp.float32
BF16 = jnp.bfloat16
UNROLL = 2


def dot(a, b, contract, precision=None):
    return lax.dot_general(
        a, b, (contract, ((), ())), precision=precision, preferred_element_type=F32
    )


def nn(a, b, precision=None):
    return dot(a, b, ((1,), (0,)), precision)


def nt(a, b, precision=None):
    return dot(a, b, ((1,), (1,)), precision)


def tn(a, b):
    return dot(a, b, ((0,), (0,)))


def split(x):
    high = x.astype(BF16)
    return high, (x - high.astype(F32)).astype(BF16)


def rows(*parts):
    return jnp.concatenate(parts, axis=0)


def lanes(*parts):
    return jnp.concatenate(parts, axis=1)


def kernel(
    size,
    width,
    q_ref, k_ref, v_ref, log_ref, gain_ref, do_ref,
    dq_ref, dk_ref, dv_ref, dlog_ref, dgain_ref,
    scratch,
):
    s = scratch
    seq_size, dp_size, levels = size
    length = q_ref.shape[0]
    pair_width = 2 * width
    pairs = q_ref.shape[1] // pair_width
    heads = 2 * pairs
    group = 2 ** levels
    chain = seq_size // group
    me = lax.axis_index("seq")
    dp = lax.axis_index("dp")

    def at_seq(index):
        return {"seq": index}

    def bit_of(value, level):
        return lax.rem(lax.div(value, 2 ** level), 2)

    def flipped(value, level):
        return value + 2 ** level * (1 - 2 * bit_of(value, level))

    place = lax.div(me, group)
    after = lax.rem(me + group, seq_size)
    before = lax.rem(me + seq_size - group, seq_size)
    seq_bits = seq_size.bit_length() - 1
    dp_bits = dp_size.bit_length() - 1
    partners = [at_seq(flipped(me, level)) for level in range(seq_bits)]
    partners += [{"dp": flipped(dp, level)} for level in range(dp_bits)]
    greeted = partners + [at_seq(after), at_seq(before)]

    barrier = pltpu.get_barrier_semaphore()
    for other in greeted:
        pl.semaphore_signal(
            barrier, inc=1, device_id=other, device_id_type=pl.DeviceIdType.MESH
        )

    def copy_to(source, target, send, recv, device):
        return pltpu.make_async_remote_copy(
            src_ref=source, dst_ref=target, send_sem=send, recv_sem=recv,
            device_id=device, device_id_type=pl.DeviceIdType.MESH,
        )

    lane_row = lax.broadcasted_iota(jnp.int32, (1, pair_width), 1)
    low_row = lane_row < width

    def low(shape):
        return lax.broadcasted_iota(jnp.int32, shape, 1) < width

    low_tok = low((length, pair_width))
    low_state = low((width, pair_width))

    def columns(pair):
        if isinstance(pair, int):
            return pl.ds(pair * pair_width, pair_width)
        return pl.ds(pl.multiple_of(pair * pair_width, pair_width), pair_width)

    def stacked(block):
        zero = jnp.zeros_like(block)
        return rows(jnp.where(low_tok, block, zero), jnp.where(low_tok, zero, block))

    def diagonal(state):
        zero = jnp.zeros_like(state)
        return rows(jnp.where(low_state, state, zero), jnp.where(low_state, zero, state))

    def packed(square):
        return jnp.where(low_state, square[:width], square[width:])

    def picked(tall):
        return jnp.where(low_tok, tall[:length], tall[length:])

    def each(start, stop, compute):
        step = UNROLL if (stop - start) % UNROLL == 0 else 1

        def body(index, carry):
            stores = []
            for offset in range(step):
                stores += compute(start + index * step + offset)
            for ref, where, value in stores:
                ref[where] = value
            return carry

        lax.fori_loop(0, (stop - start) // step, body, 0)

    ones_from = lax.broadcasted_iota(jnp.int32, (length, length), 0)
    ones_to = lax.broadcasted_iota(jnp.int32, (length, length), 1)
    causal = ones_from >= ones_to
    log_block = log_ref[...]
    s.cum[...] = nn(log_block, (ones_from <= ones_to).astype(F32), HIGH)
    cum_columns = nt(causal.astype(F32), log_block, HIGH)

    for pair in range(pairs):
        first = jnp.broadcast_to(cum_columns[:, 2 * pair:2 * pair + 1], (length, length))
        second = jnp.broadcast_to(cum_columns[:, 2 * pair + 1:2 * pair + 2], (length, length))
        s.spread[2 * pair] = first
        s.spread[2 * pair + 1] = second
        mixed = jnp.where(low_tok, first, second)
        total = mixed[length - 1:length, :]
        s.grow[pair] = jnp.exp(mixed)
        late = jnp.exp(total - mixed)
        s.late[pair] = late
        s.decay[0, pair:pair + 1, :] = jnp.exp(total)
        key = k_ref[:, columns(pair)]
        value = v_ref[:, columns(pair)].astype(F32) * late
        high, rest = split(value)
        s.fresh[pair] = packed(tn(rows(key, key), rows(high, rest)))

    pl.semaphore_wait(barrier, len(greeted))

    def scan(name, source, result, backward, works):
        x = s.scans[name]
        first_bit = 1 if backward else 0
        current, base, count = source, 0, pairs
        infos = []
        for level in range(levels):
            bit = bit_of(me, level)
            half = count // 2
            keep, give = bit * half, (1 - bit) * half
            partner = at_seq(flipped(me, level))
            copies = [
                copy_to(
                    current.at[pl.ds(give, half)], x.received[level],
                    x.up_send.at[level], x.up_recv.at[level], partner,
                )
            ]
            if not backward:
                copies.append(
                    copy_to(
                        s.decay.at[level], s.decay_other.at[level],
                        s.decay_send.at[level], s.decay_recv.at[level], partner,
                    )
                )
            for copy in copies:
                copy.start()
            works[level]()
            for copy in copies:
                copy.wait()
            if not backward:
                s.decay[level + 1] = s.decay[level] * s.decay_other[level]
            mine_first = jnp.broadcast_to(bit, (width, pair_width)) == first_bit
            mine_first_row = jnp.broadcast_to(bit, (1, pair_width)) == first_bit
            for i in range(half):
                own = current[keep + i]
                other = x.received[level][i]
                row = pl.ds(base + keep + i, 1)
                own_decay = s.decay[level, row, :]
                other_decay = s.decay_other[level, row, :]
                earlier = jnp.where(mine_first, own, other)
                later = jnp.where(mine_first, other, own)
                later_decay = jnp.where(mine_first_row, other_decay, own_decay)
                x.first[level][i] = earlier
                x.total[level][i] = later_decay * earlier + later
            infos.append((bit, half, keep, base, partner, mine_first, mine_first_row))
            current, base, count = x.total[level], base + keep, half

        start_place = chain - 1 if backward else 0
        stop_place = 0 if backward else chain - 1
        target = at_seq(before if backward else after)
        works[levels]()

        def link(i):
            return copy_to(
                x.chain_out.at[i], x.chain_in.at[i],
                x.chain_send.at[i], x.chain_recv.at[i], target,
            )

        @pl.when(place == start_place)
        def _():
            x.chain_in[...] = jnp.zeros_like(x.chain_in)

        for i in range(count):
            @pl.when(place != start_place)
            def _(i=i):
                link(i).wait_recv()

            @pl.when(place != stop_place)
            def _(i=i):
                row = pl.ds(base + i, 1)
                x.chain_out[i] = s.decay[levels, row, :] * x.chain_in[i] + current[i]
                link(i).start()

        prefix = x.chain_in
        for level in reversed(range(levels)):
            bit, half, keep, base, partner, mine_first, mine_first_row = infos[level]
            out = x.prefix[level] if level > 0 else result
            for i in range(half):
                row = pl.ds(base + keep + i, 1)
                own_decay = s.decay[level, row, :]
                other_decay = s.decay_other[level, row, :]
                first_decay = jnp.where(mine_first_row, own_decay, other_decay)
                given = prefix[i]
                moved = first_decay * given + x.first[level][i]
                x.give[level][i] = jnp.where(mine_first, moved, given)
                out[keep + i] = jnp.where(mine_first, given, moved)
            copy = copy_to(
                x.give[level], out.at[pl.ds(keep, half)],
                x.down_send.at[level], x.down_recv.at[level], partner,
            )
            copy.start()
            works[levels + 1 + levels - 1 - level]()
            copy.wait()
            prefix = out

        @pl.when(place != stop_place)
        def _():
            for i in range(count):
                link(i).wait_send()

    def inside(pair):
        query = q_ref[:, columns(pair)]
        scores = nt(query, stacked(k_ref[:, columns(pair)]))
        tables = []
        for head in range(2):
            gap = s.spread[2 * pair + head] - s.cum[pl.ds(2 * pair + head, 1), :]
            tables.append(jnp.where(causal, jnp.exp(jnp.minimum(gap, 0.0)), 0.0))
        table = lanes(*tables)
        high, rest = split(scores * table)
        values = stacked(v_ref[:, columns(pair)])
        part = nn(lanes(high, rest), rows(values, values))
        return [
            (s.table, pair, table), (s.score_high, pair, high),
            (s.score_rest, pair, rest), (s.attended, pair, part),
        ]

    def nothing():
        pass

    def cut(shares, compute):
        works, start = [], 0
        for share in shares:
            stop = min(pairs, start + share)
            if stop > start:
                works.append(functools.partial(each, start, stop, compute))
            else:
                works.append(nothing)
            start = stop
        assert start == pairs
        return works

    def shares(early, late):
        counts = [early] + [late] * (levels - 1)
        return counts + [pairs - sum(counts)] + [0] * levels

    scan("forward", s.fresh, s.start, False, cut(shares(4, 6), inside))

    s.squares[...] = jnp.zeros_like(s.squares)
    s.products[...] = jnp.zeros_like(s.products)

    def attend(pair):
        query = q_ref[:, columns(pair)]
        high, rest = split(diagonal(s.start[pair]))
        carried = nn(lanes(query, query), rows(high, rest))
        attended = s.attended[pair] + s.grow[pair] * carried
        slope = do_ref[:, columns(pair)].astype(F32) * gain_ref[pl.ds(pair, 1), :]
        return attended, slope

    def attend_pairs(index, carry):
        squares, products = s.squares[...], s.products[...]
        for offset in range(UNROLL):
            pair = index * UNROLL + offset
            attended, slope = attend(pair)
            s.attended[pair] = attended
            squares = squares + attended * attended
            products = products + attended * slope
        s.squares[...] = squares
        s.products[...] = products
        return carry

    lax.fori_loop(0, pairs // UNROLL, attend_pairs, 0)
    features = pairs * pair_width
    mean = jnp.sum(s.squares[...], axis=1, keepdims=True) / features
    inverse = 1.0 / jnp.sqrt(mean + EPSILON)
    weight = jnp.sum(s.products[...], axis=1, keepdims=True) / features * inverse * inverse * inverse
    s.inverse[...] = jnp.broadcast_to(inverse, (length, pair_width))
    s.weight[...] = jnp.broadcast_to(weight, (length, pair_width))

    def slopes(pair):
        cotangent = do_ref[:, columns(pair)].astype(F32)
        attended = s.attended[pair]
        inverse = s.inverse[...]
        gained = jnp.sum(attended * inverse * cotangent, axis=0, keepdims=True)
        slope = cotangent * gain_ref[pl.ds(pair, 1), :] * inverse - attended * s.weight[...]
        high, rest = split(slope)
        grown_high, grown_rest = split(slope * s.grow[pair])
        query = q_ref[:, columns(pair)]
        incoming = packed(tn(rows(query, query), rows(grown_high, grown_rest)))
        return [
            (s.slope_high, pair, high), (s.slope_rest, pair, rest),
            (s.incoming, pair, incoming),
            (s.gained, (0, pl.ds(pair, 1), slice(None)), gained),
        ]

    each(0, pairs, slopes)

    def gain_step(step):
        copy = copy_to(
            s.gained.at[step], s.gained_other.at[step],
            s.gain_send.at[step], s.gain_recv.at[step], partners[step],
        )
        return copy

    def gain_advance(step):
        gain_step(step).wait()
        s.gained[step + 1] = s.gained[step] + s.gained_other[step]
        if step + 1 < len(partners):
            gain_step(step + 1).start()

    gain_step(0).start()

    def grads(pair):
        query, key = q_ref[:, columns(pair)], k_ref[:, columns(pair)]
        keys, values = stacked(key), stacked(v_ref[:, columns(pair)])
        high, rest = s.slope_high[pair], s.slope_rest[pair]
        from_values = nt(lanes(high, rest), lanes(values, values))
        inner_high, inner_rest = split(from_values * s.table[pair])
        state_high, state_rest = split(diagonal(s.start[pair]))
        carried = nt(lanes(high, rest, high), lanes(state_high, state_high, state_rest))
        d_query = nn(lanes(inner_high, inner_rest), rows(keys, keys)) + s.grow[pair] * carried
        d_key = picked(tn(rows(inner_high, inner_rest), rows(query, query)))
        score_high, score_rest = s.score_high[pair], s.score_rest[pair]
        d_value = picked(tn(rows(score_high, score_rest, score_high), rows(high, high, rest)))
        return [
            (dq_ref, (slice(None), columns(pair)), d_query.astype(BF16)),
            (s.query_part, pair, d_query * query.astype(F32)),
            (s.d_key, pair, d_key), (s.d_value, pair, d_value),
        ]

    works = cut(shares(4, 6), grads)
    steps = len(partners)
    pieces = [(steps * i // len(works), steps * (i + 1) // len(works)) for i in range(len(works))]

    def with_gain(work, piece):
        def run():
            work()
            for step in range(*piece):
                gain_advance(step)
        return run

    scan("backward", s.incoming, s.end, True, [with_gain(*both) for both in zip(works, pieces)])
    dgain_ref[...] = s.gained[steps]

    s.d_cum[...] = jnp.zeros_like(s.d_cum)
    last = lax.broadcasted_iota(jnp.int32, (length, pair_width), 0) == length - 1
    head_of = lax.broadcasted_iota(jnp.int32, (heads, pair_width), 0)
    side_of = lax.broadcasted_iota(jnp.int32, (heads, pair_width), 1)

    def finish(pair):
        key, value = k_ref[:, columns(pair)], v_ref[:, columns(pair)]
        end = s.end[pair]
        high, rest = split(diagonal(end))
        late = s.late[pair]
        d_key = s.d_key[pair] + late * nt(lanes(value, value), lanes(high, rest))
        d_value = s.d_value[pair] + late * nn(lanes(key, key), rows(high, rest))
        last_state = s.decay[0, pl.ds(pair, 1), :] * s.start[pair] + s.fresh[pair]
        ended = jnp.sum(last_state * end, axis=0, keepdims=True)
        change = s.query_part[pair] - d_key * key.astype(F32)
        change = change + jnp.where(last, ended, 0.0)
        mask = (head_of == 2 * pair + (side_of >= width).astype(jnp.int32)).astype(BF16)
        change_high, change_rest = split(change)
        per_head = nt(lanes(mask, mask), lanes(change_high, change_rest))
        return d_key, d_value, per_head

    def finish_pairs(index, carry):
        total = s.d_cum[...]
        results = [finish(index * UNROLL + offset) for offset in range(UNROLL)]
        for offset, (d_key, d_value, per_head) in enumerate(results):
            pair = index * UNROLL + offset
            dk_ref[:, columns(pair)] = d_key.astype(BF16)
            dv_ref[:, columns(pair)] = d_value.astype(BF16)
            total = total + per_head
        s.d_cum[...] = total
        return carry

    lax.fori_loop(0, pairs // UNROLL, finish_pairs, 0)
    dlog_ref[...] = nn(s.d_cum[...], causal.astype(F32), HIGH)


class Bag:
    pass


def layout(length, pairs, width, levels, chained, steps):
    pair_width = 2 * width
    state = (width, pair_width)
    token = (length, pair_width)
    wide = (length, 2 * length)
    dma = pltpu.SemaphoreType.DMA

    def vmem(shape, dtype=F32):
        return pltpu.VMEM(shape, dtype)

    spec = {
        "cum": vmem((2 * pairs, length)),
        "spread": vmem((2 * pairs, length, length)),
        "grow": vmem((pairs,) + token),
        "late": vmem((pairs,) + token),
        "decay": vmem((levels + 1, pairs, pair_width)),
        "decay_other": vmem((levels, pairs, pair_width)),
        "decay_send": dma((levels,)),
        "decay_recv": dma((levels,)),
        "fresh": vmem((pairs,) + state),
        "start": vmem((pairs,) + state),
        "incoming": vmem((pairs,) + state),
        "end": vmem((pairs,) + state),
        "table": vmem((pairs,) + wide),
        "score_high": vmem((pairs,) + wide, BF16),
        "score_rest": vmem((pairs,) + wide, BF16),
        "attended": vmem((pairs,) + token),
        "squares": vmem(token),
        "products": vmem(token),
        "inverse": vmem(token),
        "weight": vmem(token),
        "slope_high": vmem((pairs,) + token, BF16),
        "slope_rest": vmem((pairs,) + token, BF16),
        "gained": vmem((steps + 1, pairs, pair_width)),
        "gained_other": vmem((steps, pairs, pair_width)),
        "gain_send": dma((steps,)),
        "gain_recv": dma((steps,)),
        "query_part": vmem((pairs,) + token),
        "d_key": vmem((pairs,) + token),
        "d_value": vmem((pairs,) + token),
        "d_cum": vmem((2 * pairs, length)),
    }
    kept = [pairs >> (level + 1) for level in range(levels)]
    for name in ("forward", "backward"):
        for level in range(levels):
            for part in ("received", "first", "total", "give"):
                spec[name, part, level] = vmem((kept[level],) + state)
            if level > 0:
                spec[name, "prefix", level] = vmem((kept[level - 1],) + state)
        spec[name, "chain_in"] = vmem((chained,) + state)
        spec[name, "chain_out"] = vmem((chained,) + state)
        for part in ("chain_send", "chain_recv"):
            spec[name, part] = dma((chained,))
        for part in ("up_send", "up_recv", "down_send", "down_recv"):
            spec[name, part] = dma((levels,))
    return spec


def gathered(keys, refs):
    bag = Bag()
    bag.scans = {"forward": Bag(), "backward": Bag()}
    for key, ref in zip(keys, refs):
        if isinstance(key, str):
            setattr(bag, key, ref)
        elif len(key) == 2:
            setattr(bag.scans[key[0]], key[1], ref)
        else:
            scan = bag.scans[key[0]]
            if not hasattr(scan, key[1]):
                setattr(scan, key[1], {})
            getattr(scan, key[1])[key[2]] = ref
    return bag


def shards(size, queries, keys, values, log_decay, gain, d_out):
    seq_size, dp_size, levels = size
    length, features = queries.shape[1:]
    heads = log_decay.shape[1]
    width = features // heads
    pairs = heads // 2
    steps = (seq_size.bit_length() - 1) + (dp_size.bit_length() - 1)
    spec = layout(length, pairs, width, levels, pairs >> levels, steps)
    names = list(spec)

    def body(*refs):
        kernel(size, width, *refs[:11], gathered(names, refs[11:]))

    whole = pl.BlockSpec(memory_space=pltpu.VMEM)
    token = jax.ShapeDtypeStruct((length, features), BF16)
    flops = 2 * heads * length * width * (12 * length + 12 * width)
    d_queries, d_keys, d_values, d_log_decay, d_gain = pl.pallas_call(
        body,
        out_shape=(
            token, token, token,
            jax.ShapeDtypeStruct((heads, length), F32),
            jax.ShapeDtypeStruct((pairs, 2 * width), F32),
        ),
        in_specs=[whole] * 6,
        out_specs=(whole,) * 5,
        scratch_shapes=list(spec.values()),
        compiler_params=pltpu.CompilerParams(
            collective_id=0, has_side_effects=True, vmem_limit_bytes=48 * 1024 * 1024
        ),
        cost_estimate=pl.CostEstimate(
            flops=flops, bytes_accessed=14 * length * features, transcendentals=0
        ),
        name="gated_backward",
    )(queries[0], keys[0], values[0], log_decay[0], gain.reshape(pairs, 2 * width), d_out[0])
    return d_queries[None], d_keys[None], d_values[None], d_log_decay[None], d_gain.reshape(-1)


def solution(mesh):
    seq_size, dp_size = mesh.shape["seq"], mesh.shape["dp"]
    levels = seq_size.bit_length() // 2
    tokens = P("dp", "seq", None)
    decays = P("dp", None, "seq")
    return jax.shard_map(
        functools.partial(shards, (seq_size, dp_size, levels)),
        mesh=mesh,
        in_specs=(tokens, tokens, tokens, decays, P(), tokens),
        out_specs=(tokens, tokens, tokens, decays, P()),
        check_vma=False,
    )
```

time: 176 us -> 70.3 us (0.40); the launches traced: 174 us -> 69.8 us
  Pallas kernels: 0 us -> 60 us
  blocking collectives: 39.9 us -> 0 us
  waiting for transfers between devices: 39.8 us -> 0 us
  matrix products: 30.7 us -> 0 us
  starting transfers between devices: 26.8 us -> 0 us
  local copies, waits for them, and re-layouts: 24.7 us -> 9.16 us
  other arithmetic: 10.6 us -> 0 us
    pallas_call x0 -> x1, Pallas kernels: none -> 60 us  [shards(): pl.pallas_call(body, out_shape=(token, token, token, jax.ShapeDtypeStruct...]
    psum x1 -> x0, blocking collectives: 39.9 us -> none  [shards(): d_gain = lax.psum(d_gain_local, ('dp', 'seq'))]
    all_to_all x5 -> x0, waiting for transfers between devices: 39.8 us -> none  [the longest x2 28.1 us: rows_prefix(): lax.all_to_all(laid, 'seq', split_axis=0, concat_axis=1, tiled=True)[0]]
    dot_general x12 -> x0, matrix products: 30.7 us -> none  [the longest x3 12.2 us: block_out(): inside = jnp.einsum('hts,hes->het', scores, values, precision=HIGH)]
    all_to_all x5 -> x0, starting transfers between devices: 26.8 us -> none  [the longest x2 10.5 us: rows_prefix(): lax.all_to_all(laid, 'seq', split_axis=0, concat_axis=1, tiled=True)[0]]
    reshape x5 -> x0, local copies, waits for them, and re-layouts: 6.79 us -> none  [the longest x3 5.34 us: rows_prefix(): laid = state.reshape(count, 1, rows, width)]
    reduce_sum x6 -> x0, other arithmetic: 4.61 us -> none  [the longest x1 1.69 us: block_out(): return inside + jnp.exp(cumulative)[:, None, :] * carried]
    slice x12 -> x0, local copies, waits for them, and re-layouts: 3.93 us -> none  [the longest x9 3.9 us: running(): states[:-hop]]
  transfers between devices with their start and end apart: 5 -> 0, of which waited for: 3 -> 0; matrix products, arithmetic and copies ran while one was open for 13% -> 0% of each run, Pallas kernels for 0% -> 0%
where the time goes in v1:
time: 70.3 us; the launch traced here: 69.8 us
  Pallas kernels  60 us (85%)
  local copies, waits for them, and re-layouts  9.16 us (13%)
    pallas_call x1, Pallas kernels, shards(): pl.pallas_call(body, out_shape=(token, token, token, jax.ShapeDtypeStruct...  60 us
    unnamed x17, local copies, waits for them, and re-layouts  9.16 us

profile of v1, /device:TPU:1, one launch (start us, length us, event | category | flops | bytes accessed | tf_op | source)
XLA Modules:
  0.0 69.8 jit_solution(14268484311375071666)
XLA Ops:
  0.6 0.0 copy-start.5
  0.6 0.7 copy-done.5
  1.3 0.0 copy-start
  1.3 1.0 %copy-done = bf16[1,128,2048]{2,1,0:T(8,128)(2,1)S(1)} copy-done((bf16[1,128,2048]{2,1,0:T(8,128)(2,1)S(1)}, bf16[1,128,2048]{2,1,0:T(8,128)(2,1)}, u32[]{:S(2)}) %copy-start) | copy-done | bytes 524312
  2.4 0.0 copy-start.1
  2.4 1.0 %copy-done.1 = bf16[1,128,2048]{2,1,0:T(8,128)(2,1)S(1)} copy-done((bf16[1,128,2048]{2,1,0:T(8,128)(2,1)S(1)}, bf16[1,128,2048]{2,1,0:T(8,128)(2,1)}, u32[]{:S(2)}) %copy-start.1) | copy-done | bytes 524312
  3.4 0.0 copy-start.2
  3.4 1.0 %copy-done.2 = bf16[1,128,2048]{2,1,0:T(8,128)(2,1)S(1)} copy-done((bf16[1,128,2048]{2,1,0:T(8,128)(2,1)S(1)}, bf16[1,128,2048]{2,1,0:T(8,128)(2,1)}, u32[]{:S(2)}) %copy-start.2) | copy-done | bytes 524312
  4.5 0.0 copy-start.3
  4.5 1.0 %copy-done.3 = bf16[1,128,2048]{2,1,0:T(8,128)(2,1)S(1)} copy-done((bf16[1,128,2048]{2,1,0:T(8,128)(2,1)S(1)}, bf16[1,128,2048]{2,1,0:T(8,128)(2,1)}, u32[]{:S(2)}) %copy-start.3) | copy-done | bytes 524312
  5.5 0.0 copy-start.4
  5.5 0.7 %copy-done.4 = f32[1,32,128]{2,1,0:T(8,128)S(1)} copy-done((f32[1,32,128]{2,1,0:T(8,128)S(1)}, f32[1,32,128]{2,1,0:T(8,128)}, u32[]{:S(2)}) %copy-start.4) | copy-done | bytes 16408
  6.2 60.0 %gated_backward.1 = (bf16[128,2048]{1,0:T(8,128)(2,1)S(1)}, bf16[128,2048]{1,0:T(8,128)(2,1)S(1)}, bf16[128,2048]{1,0:T(8,128)(2,1)S(1)}, f32[32,128]{1,0:T(8,128)S(1)}, f32[16,128]{1,0:T(8,128)S(1)}) custom-call(bf16[128,2048]{1,0:T(8,128)(2,1)S(1)} %bitcast.16, bf16[128,2048]{1,0:T(8,128)(2,1)S(1)} %bitcast.17, bf16[128,2048]{1,0:T(8,128)(2,1)S(1)} %bitcast.18, ...), custom_call_target="tpu_custom_call" | custom-call | flops 1207959552 | bytes 3670016 | tf_op jit(solution)/shard_map/gated_backward/pallas_call | solution.py:524
  66.2 0.8 %copy.16 = bf16[1,128,2048]{2,1,0:T(8,128)(2,1)} copy(bf16[1,128,2048]{2,1,0:T(8,128)(2,1)S(1)} %bitcast.13) | data formatting | bytes 1048576
  67.0 0.8 %copy.17 = bf16[1,128,2048]{2,1,0:T(8,128)(2,1)} copy(bf16[1,128,2048]{2,1,0:T(8,128)(2,1)S(1)} %bitcast.12) | data formatting | bytes 1048576
  67.8 0.8 %copy.18 = bf16[1,128,2048]{2,1,0:T(8,128)(2,1)} copy(bf16[1,128,2048]{2,1,0:T(8,128)(2,1)S(1)} %bitcast.11) | data formatting | bytes 1048576
  68.6 0.6 copy.19
  69.2 0.6 copy.20
Async XLA Ops:
  0.6 0.7 %copy-start.5 = (f32[2048]{0:T(1024)S(1)}, f32[2048]{0:T(1024)}, u32[]{:S(2)}) copy-start(f32[2048]{0:T(1024)} %param.10) | copy-start | bytes 24580
  1.3 1.0 %copy-start = (bf16[1,128,2048]{2,1,0:T(8,128)(2,1)S(1)}, bf16[1,128,2048]{2,1,0:T(8,128)(2,1)}, u32[]{:S(2)}) copy-start(bf16[1,128,2048]{2,1,0:T(8,128)(2,1)} %param.6) | copy-start | bytes 1572868
  2.4 1.0 %copy-start.1 = (bf16[1,128,2048]{2,1,0:T(8,128)(2,1)S(1)}, bf16[1,128,2048]{2,1,0:T(8,128)(2,1)}, u32[]{:S(2)}) copy-start(bf16[1,128,2048]{2,1,0:T(8,128)(2,1)} %param.7) | copy-start | bytes 1572868
  3.4 1.0 %copy-start.2 = (bf16[1,128,2048]{2,1,0:T(8,128)(2,1)S(1)}, bf16[1,128,2048]{2,1,0:T(8,128)(2,1)}, u32[]{:S(2)}) copy-start(bf16[1,128,2048]{2,1,0:T(8,128)(2,1)} %param.8) | copy-start | bytes 1572868
  4.5 1.0 %copy-start.3 = (bf16[1,128,2048]{2,1,0:T(8,128)(2,1)S(1)}, bf16[1,128,2048]{2,1,0:T(8,128)(2,1)}, u32[]{:S(2)}) copy-start(bf16[1,128,2048]{2,1,0:T(8,128)(2,1)} %param.11) | copy-start | bytes 1572868
  5.5 0.7 %copy-start.4 = (f32[1,32,128]{2,1,0:T(8,128)S(1)}, f32[1,32,128]{2,1,0:T(8,128)}, u32[]{:S(2)}) copy-start(f32[1,32,128]{2,1,0:T(8,128)} %param.9) | copy-start | bytes 49156
